TPU v7x, 32 devices: a whole 2x2x4 slice. The times are simulated.
32 devices in a mesh: section: 2 (over y), dp: 4 (over z), tensor: 4 (over x, core).
Axes of the slice: x: 2, y: 2, z: 4, core: 2. Of those that a mesh axis runs over, the one named last changes fastest.
Arguments:
- layer_input: bfloat16 [2, 2, 256, 8192], P('section', None, 'tensor', 'dp'), may hold values from -64 to 64
- ready_grad: bfloat16 [2, 256, 8192], P('section', 'tensor', 'dp'), may hold values from -6 to 6
- late_grad: bfloat16 [256, 8192], P('tensor', 'dp'), may hold values from -6 to 6
- norm_gain: float32 [2, 8192], P('section', 'dp'), may hold values from 0.25 to 4.5
- norm_bias: float32 [2, 8192], P('section', 'dp'), may hold values from -3 to 3
- up_weight: bfloat16 [2, 8192, 16384], P('section', 'dp', 'tensor'), may hold values from -0.0625 to 0.0625
- down_weight: bfloat16 [2, 16384, 8192], P('section', 'tensor', 'dp'), may hold values from -0.046875 to 0.046875
Outputs:
- input_grad: bfloat16 [2, 2, 256, 8192], P('section', None, 'tensor', 'dp')
- up_grad: bfloat16 [2, 8192, 16384], P('section', 'dp', 'tensor')
- down_grad: bfloat16 [2, 16384, 8192], P('section', 'tensor', 'dp')
- gain_grad: float32 [2, 8192], P('section', 'dp')
- bias_grad: float32 [2, 8192], P('section', 'dp')
All inputs are finite; a program needn't handle non-finite values.
Results may differ from a plain program's by a relative error of at most 0.03.
Values may be sent and summed in bfloat16 or wider, within the bound.
A program may use at most 192 MiB of HBM per device.

v0:
```python
import math

import jax
import jax.numpy as jnp
from jax import lax
from jax.sharding import PartitionSpec as P

MODEL_WIDTH = 8192


epsilon = 1e-05
inv_root_two = 0.7071067811865476
inv_root_two_pi = 0.3989422804014327


def from_behind(block, axis, distance):
    devices = range(lax.axis_size(axis))
    route = [(i - distance, i) for i in devices if i - distance in devices]
    return lax.ppermute(block, axis, route)


def gelu_value(values):
    return 0.5 * values * (1.0 + lax.erf(values * inv_root_two))


def gelu_slope(values):
    return (
        0.5 * (1.0 + lax.erf(values * inv_root_two))
        + values * jnp.exp(-0.5 * values * values) * inv_root_two_pi
    )


def round_partial(partial_value):
    return lax.optimization_barrier(partial_value.astype(jnp.bfloat16)).astype(jnp.float32)


def section_pass(inputs_tile, incoming_gradient, scale_gain, shift_bias, weight_up, weight_down):
    tensor_rows = inputs_tile.shape[0]
    inputs_float = inputs_tile.astype(jnp.float32)
    row_total, row_squares = lax.psum(
        (
            jnp.sum(inputs_float, axis=1, keepdims=True),
            jnp.sum(inputs_float * inputs_float, axis=1, keepdims=True),
        ),
        "dp",
    )
    row_mean = row_total / MODEL_WIDTH
    variance = row_squares / MODEL_WIDTH - row_mean * row_mean
    inverse_deviation = lax.rsqrt(variance + epsilon)
    centered_input = (inputs_float - row_mean) * inverse_deviation
    normalized = (centered_input * scale_gain + shift_bias).astype(jnp.bfloat16)
    normed_all = lax.all_gather(normalized, "tensor", axis=0, tiled=True)
    left_rows = normed_all
    pre_rows = lax.psum_scatter(
        round_partial(jnp.dot(left_rows, weight_up, preferred_element_type=jnp.float32)).astype(
            jnp.bfloat16
        ),
        "dp",
        scatter_dimension=0,
        tiled=True,
    ).astype(jnp.float32)
    act_all = lax.all_gather(gelu_value(pre_rows).astype(jnp.bfloat16), "dp", axis=0, tiled=True)
    slope = gelu_slope(pre_rows)
    down_term = jnp.dot(act_all.T, incoming_gradient, preferred_element_type=jnp.float32)
    left_rows = incoming_gradient
    act_grad = lax.psum_scatter(
        round_partial(
            lax.dot_general(
                left_rows, weight_down, (((1,), (1,)), ((), ())), preferred_element_type=jnp.float32
            )
        ).astype(jnp.bfloat16),
        "dp",
        scatter_dimension=0,
        tiled=True,
    ).astype(jnp.float32)
    pre_grad = (act_grad * slope).astype(jnp.bfloat16)
    pre_grad_all = lax.all_gather(pre_grad, "dp", axis=0, tiled=True)
    up_term = jnp.dot(normed_all.T, pre_grad_all, preferred_element_type=jnp.float32)
    left_rows = pre_grad_all
    normalized_gradient = lax.psum_scatter(
        lax.dot_general(
            left_rows, weight_up, (((1,), (1,)), ((), ())), preferred_element_type=jnp.float32
        ).astype(jnp.bfloat16),
        "tensor",
        scatter_dimension=0,
        tiled=True,
    ).astype(jnp.float32)
    gain_product = jnp.sum(normalized_gradient * centered_input, axis=0)
    bias_term = jnp.sum(normalized_gradient, axis=0)
    centered_gradient = normalized_gradient * scale_gain
    centered_total, centered_cross = lax.psum(
        (
            jnp.sum(centered_gradient, axis=1, keepdims=True),
            jnp.sum(centered_gradient * centered_input, axis=1, keepdims=True),
        ),
        "dp",
    )
    local_rows = lax.dynamic_slice_in_dim(
        incoming_gradient, lax.axis_index("tensor") * tensor_rows, tensor_rows, 0
    ).astype(jnp.float32)
    final_output = local_rows + inverse_deviation * (
        centered_gradient
        - centered_total / MODEL_WIDTH
        - centered_input * (centered_cross / MODEL_WIDTH)
    )
    return (final_output.astype(jnp.bfloat16), down_term, up_term, gain_product, bias_term)


def body(layer_input, ready_grad, late_grad, norm_gain, norm_bias, up_weight, down_weight):
    early = lax.axis_index("section") == 0
    scale_gain = norm_gain[0]
    shift_bias = norm_bias[0]
    weight_up = up_weight[0]
    weight_down = down_weight[0]
    ready_whole, late_whole = (
        lax.all_gather(ready_grad[0], "tensor", axis=0, tiled=True),
        lax.all_gather(late_grad, "tensor", axis=0, tiled=True),
    )
    first_pass = section_pass(
        layer_input[0, 0], ready_whole, scale_gain, shift_bias, weight_up, weight_down
    )
    sent = first_pass[0]
    assembled = lax.all_gather(sent, "tensor", axis=0, tiled=True)
    arrived = from_behind(assembled, "section", -1)
    second_incoming = jnp.where(early, arrived, late_whole)
    second_pass = section_pass(
        layer_input[0, 1], second_incoming, scale_gain, shift_bias, weight_up, weight_down
    )
    scale = 1.0 / math.sqrt(2 * second_incoming.shape[0])
    down_part = ((first_pass[1] + second_pass[1]) * scale).astype(jnp.bfloat16)
    up_part = ((first_pass[2] + second_pass[2]) * scale).astype(jnp.bfloat16)
    gain_sum, bias_sum = lax.psum(
        (first_pass[3] + second_pass[3], first_pass[4] + second_pass[4]), "tensor"
    )
    results = jnp.stack([first_pass[0], second_pass[0]])
    return (
        results[None],
        up_part[None],
        down_part[None],
        (gain_sum * scale)[None],
        (bias_sum * scale)[None],
    )


def solution(mesh):
    in_specs = (
        P("section", None, "tensor", "dp"),
        P("section", "tensor", "dp"),
        P("tensor", "dp"),
        P("section", "dp"),
        P("section", "dp"),
        P("section", "dp", "tensor"),
        P("section", "tensor", "dp"),
    )
    out_specs = (
        P("section", None, "tensor", "dp"),
        P("section", "dp", "tensor"),
        P("section", "tensor", "dp"),
        P("section", "dp"),
        P("section", "dp"),
    )
    return jax.shard_map(body, mesh=mesh, in_specs=in_specs, out_specs=out_specs, check_vma=False)
```

profile of v0, /device:TPU:0, one launch (start us, length us, event | category | flops | bytes accessed | tf_op | source)
XLA Modules:
  0.0 594.8 jit_solution(13825570276484820397)
XLA Ops:
  9.5 13.5 %all-reduce.3 = (f32[64,1]{0,1:T(1,128)S(1)}, f32[64,1]{0,1:T(1,128)S(1)}) all-reduce(f32[64,1]{0,1:T(1,128)S(1)} %bitcast.170, f32[64,1]{0,1:T(1,128)S(1)} %bitcast.167), channel_id=1, replica_groups=mesh['section'=2,'dp'=4,'tensor'=4] {'dp'}, use_global_device_ids=true, to_apply=%region_3.0 | all-reduce | flops 128 | bytes 1024 | tf_op jit(solution)/shard_map/psum | solution.py:40
  25.7 14.3 %all-gather.11.cloned.1.call-done = bf16[256,2048]{1,0:T(8,128)(2,1)} async-done(((bf16[64,2048]{1,0:T(8,128)(2,1)}), bf16[256,2048]{1,0:T(8,128)(2,1)}) %all-gather.11.cloned.1.call-update) | async-done | bytes 1048592 | tf_op jit(solution)/shard_map/all_gather | solution.py:52
  40.0 11.9 %fusion.20 = bf16[256,4096]{1,0:T(8,128)(2,1)} fusion(bf16[256,2048]{1,0:T(8,128)(2,1)} %all-gather.11.cloned.1.call-done, bf16[1,2048,4096]{2,1,0:T(8,128)(2,1)} %param.12), kind=kOutput, calls=%fused_computation.18 | convolution fusion | flops 4296015872 | bytes 19922944 | tf_op jit(solution)/shard_map/dot_general | solution.py:55
  58.3 12.0 %fusion.14 = bf16[256,4096]{1,0:T(8,128)(2,1)} fusion(bf16[1,4096,2048]{2,1,0:T(8,128)(2,1)} %param.13, bf16[1,256,2048]{2,1,0:T(8,128)(2,1)} %all-gather.27.cloned.1.call-done), kind=kOutput, calls=%fused_computation.16 | convolution fusion | flops 4296015872 | bytes 19922944 | tf_op jit(solution)/shard_map/dot_general | solution.py:68
  70.3 34.7 %reduce-scatter.9.cloned.1.call-done = bf16[64,4096]{1,0:T(8,128)(2,1)} async-done(((bf16[256,4096]{1,0:T(8,128)(2,1)}), bf16[64,4096]{1,0:T(8,128)(2,1)}) %reduce-scatter.9.cloned.1.call-update) | async-done | bytes 524304 | tf_op jit(solution)/shard_map/reduce_scatter | solution.py:54
  105.1 46.1 %reduce-scatter.7.cloned.1.call-done = bf16[64,4096]{1,0:T(8,128)(2,1)} async-done(((bf16[256,4096]{1,0:T(8,128)(2,1)}), bf16[64,4096]{1,0:T(8,128)(2,1)}) %reduce-scatter.7.cloned.1.call-update) | async-done | bytes 524304 | tf_op jit(solution)/shard_map/reduce_scatter | solution.py:66
  154.1 45.2 %all-gather.13.cloned.1.call-done = bf16[256,4096]{1,0:T(8,128)(2,1)} async-done(((bf16[64,4096]{1,0:T(8,128)(2,1)}), bf16[256,4096]{1,0:T(8,128)(2,1)}) %all-gather.13.cloned.1.call-update) | async-done | bytes 2097168 | tf_op jit(solution)/shard_map/all_gather | solution.py:77
  199.3 11.9 %fusion.26 = bf16[256,2048]{1,0:T(8,128)(2,1)} fusion(bf16[256,4096]{1,0:T(8,128)(2,1)} %all-gather.13.cloned.1.call-done, bf16[1,2048,4096]{2,1,0:T(8,128)(2,1)} %param.12), kind=kOutput, calls=%fused_computation.20 | convolution fusion | flops 4295491584 | bytes 19922944 | tf_op jit(solution)/shard_map/dot_general | solution.py:81
  211.3 23.7 %reduce-scatter.11.cloned.1.call-done = bf16[64,2048]{1,0:T(8,128)(2,1)} async-done(((bf16[256,2048]{1,0:T(8,128)(2,1)}), bf16[64,2048]{1,0:T(8,128)(2,1)}) %reduce-scatter.11.cloned.1.call-update) | async-done | bytes 262160 | tf_op jit(solution)/shard_map/reduce_scatter | solution.py:80
  251.7 12.6 %all-gather.19.cloned.1.call-done = bf16[256,2048]{1,0:T(8,128)(2,1)} async-done(((bf16[64,2048]{1,0:T(8,128)(2,1)}), bf16[256,2048]{1,0:T(8,128)(2,1)}) %all-gather.19.cloned.1.call-update) | async-done | bytes 1048592 | tf_op jit(solution)/shard_map/all_gather | solution.py:52
  264.3 11.9 %fusion.23 = bf16[256,4096]{1,0:T(8,128)(2,1)} fusion(bf16[256,2048]{1,0:T(8,128)(2,1)} %all-gather.19.cloned.1.call-done, bf16[1,2048,4096]{2,1,0:T(8,128)(2,1)} %param.12), kind=kOutput, calls=%fused_computation.19 | convolution fusion | flops 4296015872 | bytes 19922944 | tf_op jit(solution)/shard_map/dot_general | solution.py:55
  284.2 16.9 %all-gather.17.cloned.1.call-done = bf16[256,2048]{1,0:T(8,128)(2,1)} async-done(((bf16[64,2048]{1,0:T(8,128)(2,1)}), bf16[256,2048]{1,0:T(8,128)(2,1)}) %all-gather.17.cloned.1.call-update) | async-done | bytes 1048592 | tf_op jit(solution)/shard_map/all_gather | solution.py:117
  311.6 18.1 %fusion.17 = bf16[256,4096]{1,0:T(8,128)(2,1)} fusion(bf16[256,2048]{1,0:T(8,128)(2,1)S(1)} %broadcast_select_fusion, bf16[1,4096,2048]{2,1,0:T(8,128)(2,1)} %param.13), kind=kOutput, calls=%fused_computation.17 | convolution fusion | flops 4296015872 | bytes 19922944 | tf_op jit(solution)/shard_map/dot_general | solution.py:68
  330.3 17.5 %reduce-scatter.15.cloned.1.call-done = bf16[64,4096]{1,0:T(8,128)(2,1)} async-done(((bf16[256,4096]{1,0:T(8,128)(2,1)}), bf16[64,4096]{1,0:T(8,128)(2,1)}) %reduce-scatter.15.cloned.1.call-update) | async-done | bytes 524304 | tf_op jit(solution)/shard_map/reduce_scatter | solution.py:54
  347.9 46.1 %reduce-scatter.13.cloned.1.call-done = bf16[64,4096]{1,0:T(8,128)(2,1)} async-done(((bf16[256,4096]{1,0:T(8,128)(2,1)}), bf16[64,4096]{1,0:T(8,128)(2,1)}) %reduce-scatter.13.cloned.1.call-update) | async-done | bytes 524304 | tf_op jit(solution)/shard_map/reduce_scatter | solution.py:66
  397.3 17.7 %fusion.88 = f32[2048,4096]{1,0:T(8,128)} fusion(bf16[256,2048]{1,0:T(8,128)(2,1)} %all-gather.11.cloned.1.call-done, bf16[256,4096]{1,0:T(8,128)(2,1)} %all-gather.13.cloned.1.call-done), kind=kOutput, calls=%fused_computation.110 | convolution fusion | flops 4294967296 | bytes 36700160 | tf_op jit(solution)/shard_map/dot_general | solution.py:78
  415.0 26.3 %all-gather.23.cloned.1.call-done = bf16[256,4096]{1,0:T(8,128)(2,1)} async-done(((bf16[64,4096]{1,0:T(8,128)(2,1)}), bf16[256,4096]{1,0:T(8,128)(2,1)}) %all-gather.23.cloned.1.call-update) | async-done | bytes 2097168 | tf_op jit(solution)/shard_map/all_gather | solution.py:62
  441.3 15.5 %fusion.51 = f32[4096,2048]{1,0:T(8,128)} fusion(bf16[256,4096]{1,0:T(8,128)(2,1)} %all-gather.23.cloned.1.call-done, bf16[1,256,2048]{2,1,0:T(8,128)(2,1)S(1)} %copy-done.2), kind=kOutput, calls=%fused_computation.51 | convolution fusion | flops 4294967296 | bytes 36700160 | tf_op jit(solution)/shard_map/dot_general | solution.py:64
  456.8 31.5 %all-gather.21.cloned.1.call-done = bf16[256,4096]{1,0:T(8,128)(2,1)} async-done(((bf16[64,4096]{1,0:T(8,128)(2,1)}), bf16[256,4096]{1,0:T(8,128)(2,1)}) %all-gather.21.cloned.1.call-update) | async-done | bytes 2097168 | tf_op jit(solution)/shard_map/all_gather | solution.py:77
  488.2 11.9 %fusion.29 = bf16[256,2048]{1,0:T(8,128)(2,1)} fusion(bf16[256,4096]{1,0:T(8,128)(2,1)} %all-gather.21.cloned.1.call-done, bf16[1,2048,4096]{2,1,0:T(8,128)(2,1)} %param.12), kind=kOutput, calls=%fused_computation.21 | convolution fusion | flops 4295491584 | bytes 19922944 | tf_op jit(solution)/shard_map/dot_general | solution.py:81
  500.2 17.7 %fusion = bf16[1,2048,4096]{2,1,0:T(8,128)(2,1)} fusion(f32[2048,4096]{1,0:T(8,128)} %fusion.88, bf16[256,2048]{1,0:T(8,128)(2,1)S(1)} %copy-done.3, bf16[256,4096]{1,0:T(8,128)(2,1)} %all-gather.21.cloned.1.call-done), kind=kOutput, calls=%fused_computation.2 | convolution fusion | flops 4320133120 | bytes 53477376 | tf_op jit(solution)/shard_map/dot_general | solution.py:78
  517.8 17.2 %all-gather.25.cloned.1.call-done = bf16[256,4096]{1,0:T(8,128)(2,1)} async-done(((bf16[64,4096]{1,0:T(8,128)(2,1)}), bf16[256,4096]{1,0:T(8,128)(2,1)}) %all-gather.25.cloned.1.call-update) | async-done | bytes 2097168 | tf_op jit(solution)/shard_map/all_gather | solution.py:62
  535.0 17.7 %fusion.1 = bf16[1,4096,2048]{2,1,0:T(8,128)(2,1)} fusion(f32[4096,2048]{1,0:T(8,128)} %fusion.51, bf16[256,4096]{1,0:T(8,128)(2,1)} %all-gather.25.cloned.1.call-done, bf16[256,2048]{1,0:T(8,128)(2,1)S(1)} %broadcast_select_fusion), kind=kOutput, calls=%fused_computation.3 | convolution fusion | flops 4320133120 | bytes 53477376 | tf_op jit(solution)/shard_map/dot_general | solution.py:64
  562.5 11.7 %all-reduce.1 = (f32[64,1]{0,1:T(1,128)S(1)}, f32[64,1]{0,1:T(1,128)S(1)}) all-reduce(f32[64,1]{0,1:T(1,128)S(1)} %bitcast.168, f32[64,1]{0,1:T(1,128)S(1)} %bitcast.169), channel_id=1, replica_groups=mesh['section'=2,'dp'=4,'tensor'=4] {'dp'}, use_global_device_ids=true, to_apply=%region_21.22 | all-reduce | flops 128 | bytes 1024 | tf_op jit(solution)/shard_map/psum | solution.py:91
  (69 shorter events, 77.0 us)
Async XLA Ops:
  7.2 32.8 %all-gather.11.cloned.1.call-start = ((), (), s32[]{:S(2)}) async-start(), calls=%async_computation.7 | async-start | bytes 1310720 | tf_op jit(solution)/shard_map/all_gather | solution.py:52
  24.9 33.4 %all-gather.27.cloned.1.call-start = ((), (), s32[]{:S(2)}) async-start(), calls=%async_computation.20 | async-start | bytes 1310720 | tf_op jit(solution)/shard_map/all_gather | solution.py:116
  25.6 79.4 %reduce-scatter.9.cloned.1.call-start = ((), (), s32[]{:S(2)}) async-start(), calls=%async_computation.8 | async-start | bytes 2621440 | tf_op jit(solution)/shard_map/reduce_scatter | solution.py:54
  51.9 99.2 %reduce-scatter.7.cloned.1.call-start = ((), (), s32[]{:S(2)}) async-start(), calls=%async_computation.6 | async-start | bytes 2621440 | tf_op jit(solution)/shard_map/reduce_scatter | solution.py:66
  70.3 164.8 %copy-start = (bf16[1,2,64,2048]{3,2,1,0:T(8,128)(2,1)S(1)}, bf16[1,2,64,2048]{3,2,1,0:T(8,128)(2,1)}, u32[]{:S(2)}) copy-start(bf16[1,2,64,2048]{3,2,1,0:T(8,128)(2,1)} %param.7) | copy-start | bytes 1572868
  70.3 164.7 %copy-start.4 = (f32[1,2048]{1,0:T(1,128)S(1)}, f32[1,2048]{1,0:T(1,128)}, u32[]{:S(2)}) copy-start(f32[1,2048]{1,0:T(1,128)} %param.10) | copy-start | bytes 24580
  70.3 129.0 %all-gather.13.cloned.1.call-start = ((), (), s32[]{:S(2)}) async-start(), calls=%async_computation.9 | async-start | bytes 2621440 | tf_op jit(solution)/shard_map/all_gather | solution.py:77
  153.9 94.2 %copy-start.2 = (bf16[1,256,2048]{2,1,0:T(8,128)(2,1)S(1)}, bf16[1,256,2048]{2,1,0:T(8,128)(2,1)}, u32[]{:S(2)}) copy-start(bf16[1,256,2048]{2,1,0:T(8,128)(2,1)} %all-gather.27.cloned.1.call-done) | copy-start | bytes 3145732
  153.9 94.2 %copy-start.5 = (f32[1,2048]{1,0:T(1,128)S(1)}, f32[1,2048]{1,0:T(1,128)}, u32[]{:S(2)}) copy-start(f32[1,2048]{1,0:T(1,128)} %param.11) | copy-start | bytes 24580
  153.9 81.1 %reduce-scatter.11.cloned.1.call-start = ((), (), s32[]{:S(2)}) async-start(), calls=%async_computation.10 | async-start | bytes 1310720 | tf_op jit(solution)/shard_map/reduce_scatter | solution.py:80
  211.3 53.1 %all-gather.19.cloned.1.call-start = ((), (), s32[]{:S(2)}) async-start(), calls=%async_computation.14 | async-start | bytes 1310720 | tf_op jit(solution)/shard_map/all_gather | solution.py:52
  250.2 32.5 %all-gather.15.cloned.1.call-start = ((), (), s32[]{:S(2)}) async-start(), calls=%async_computation.11 | async-start | bytes 1310720 | tf_op jit(solution)/shard_map/all_gather | solution.py:123
  251.0 50.2 %all-gather.17.cloned.1.call-start = ((), (), s32[]{:S(2)}) async-start(), calls=%async_computation.12 | async-start | bytes 1310720 | tf_op jit(solution)/shard_map/all_gather | solution.py:117
  251.7 96.2 %reduce-scatter.15.cloned.1.call-start = ((), (), s32[]{:S(2)}) async-start(), calls=%async_computation.15 | async-start | bytes 2621440 | tf_op jit(solution)/shard_map/reduce_scatter | solution.py:54
  276.3 117.7 %reduce-scatter.13.cloned.1.call-start = ((), (), s32[]{:S(2)}) async-start(), calls=%async_computation.13 | async-start | bytes 2621440 | tf_op jit(solution)/shard_map/reduce_scatter | solution.py:66
  282.7 27.5 %collective-permute-start = (bf16[256,2048]{1,0:T(8,128)(2,1)}, bf16[256,2048]{1,0:T(8,128)(2,1)}, u32[]{:S(2)}, u32[]{:S(2)}) collective-permute-start(bf16[256,2048]{1,0:T(8,128)(2,1)} %all-gather.15.cloned.1.call-done), channel_id=1, source_target_pairs={{16,0},{17,1},{18,2},{19,3},{20,4},{21,5},{22,6},{23,7},{24,8},{25... | collective-permute-start | bytes 3145736 | tf_op jit(solution)/shard_map/ppermute | solution.py:19
  329.7 111.6 %all-gather.23.cloned.1.call-start = ((), (), s32[]{:S(2)}) async-start(), calls=%async_computation.18 | async-start | bytes 2621440 | tf_op jit(solution)/shard_map/all_gather | solution.py:62
  330.3 158.0 %all-gather.21.cloned.1.call-start = ((), (), s32[]{:S(2)}) async-start(), calls=%async_computation.16 | async-start | bytes 2621440 | tf_op jit(solution)/shard_map/all_gather | solution.py:77
  396.7 138.3 %all-gather.25.cloned.1.call-start = ((), (), s32[]{:S(2)}) async-start(), calls=%async_computation.19 | async-start | bytes 2621440 | tf_op jit(solution)/shard_map/all_gather | solution.py:62
  397.3 163.9 %reduce-scatter.17.cloned.1.call-start = ((), (), s32[]{:S(2)}) async-start(), calls=%async_computation.17 | async-start | bytes 1310720 | tf_op jit(solution)/shard_map/reduce_scatter | solution.py:80
  456.8 43.4 %copy-start.3 = (bf16[256,2048]{1,0:T(8,128)(2,1)S(1)}, bf16[256,2048]{1,0:T(8,128)(2,1)}, u32[]{:S(2)}) copy-start(bf16[256,2048]{1,0:T(8,128)(2,1)} %all-gather.19.cloned.1.call-done) | copy-start | bytes 3145732
  517.8 69.2 %copy-start.1 = (bf16[64,2048]{1,0:T(8,128)(2,1)S(1)}, bf16[64,2048]{1,0:T(8,128)(2,1)}, u32[]{:S(2)}) copy-start(bf16[64,2048]{1,0:T(8,128)(2,1)} %get-tuple-element.26) | copy-start | bytes 786436
Sparse Core Ops, SparseCore 0:
  25.0 14.9 all-gather.10
  41.5 16.7 all-gather.26
  61.2 43.8 reduce-scatter.8
  107.9 43.1 reduce-scatter.6
  154.0 45.2 all-gather.12
  211.4 23.5 reduce-scatter.10
  250.3 13.9 all-gather.18
  266.0 16.7 all-gather.14
  284.4 16.7 all-gather.16
  303.9 43.8 reduce-scatter.14
  350.7 43.1 reduce-scatter.12
  396.0 45.2 all-gather.22
  443.5 44.6 all-gather.20
  490.3 44.6 all-gather.24
  537.5 23.5 reduce-scatter.16
where the time goes:
time: 602 us; the launch traced here: 595 us
  waiting for transfers between devices  366 us (61%)
  matrix products  146 us (24%)
  blocking collectives  47.1 us (8%)
  other arithmetic  19.2 us (3%)
  between operations  14.5 us (2%)
    reduce_scatter x2, waiting for transfers between devices, section_pass(): lax.psum_scatter(round_partial(lax.dot_general(left_rows, weight_down, ((...  92.1 us
    all_gather x2, waiting for transfers between devices, section_pass(): pre_grad_all = lax.all_gather(pre_grad, 'dp', axis=0, tiled=True)  76.7 us
    reduce_scatter x2, waiting for transfers between devices, section_pass(): lax.psum_scatter(round_partial(jnp.dot(left_rows, weight_up, preferred_el...  52.3 us
    all_gather x2, waiting for transfers between devices, section_pass(): lax.all_gather(gelu_value(pre_rows).astype(jnp.bfloat16), 'dp', axis=0, t...  43.5 us
    dot_general x2, matrix products, section_pass(): jnp.dot(normed_all.T, pre_grad_all, preferred_element_type=jnp.float32)  35.3 us
    dot_general x2, matrix products, section_pass(): jnp.dot(act_all.T, incoming_gradient, preferred_element_type=jnp.float32)  33.2 us
    reduce_scatter x2, waiting for transfers between devices, section_pass(): lax.psum_scatter(lax.dot_general(left_rows, weight_up, (((1,), (1,)), (()...  32.1 us
    dot_general x2, matrix products, section_pass(): lax.dot_general(left_rows, weight_down, (((1,), (1,)), ((), ())), preferr...  30 us
  transfers between devices with their start and end apart: 16, of which 16 were waited for; matrix products, arithmetic and copies ran while one was open for 23% of the time, Pallas kernels for 0%

commit v1 on v0

v1 whole, which is shorter than its diff:
```python
import functools
import math

import jax
import jax.numpy as jnp
from jax import lax
from jax.experimental import pallas as pl
from jax.experimental.pallas import tpu as pltpu
from jax.sharding import PartitionSpec as P

MODEL_WIDTH = 8192
MESH = pl.DeviceIdType.MESH

epsilon = 1e-05
inv_root_two = 0.7071067811865476
inv_root_two_pi = 0.3989422804014327


def relay_kernel(kind, n, *refs):
    has_pre, has_act = kind != "grad", kind != "value"
    it = iter(refs)
    norm_ref = next(it) if has_pre else None
    inc_ref = next(it) if has_act else None
    slope_ref = next(it) if kind == "grad" else None
    up_hbm = next(it)
    down_hbm = next(it) if has_act else None
    act_ref = next(it) if has_pre else None
    slope_out = next(it) if kind == "value" else None
    pg_ref, ng_ref = (next(it), next(it)) if has_act else (None, None)
    up_v, up_sem = next(it), next(it)
    down_v, down_sem = (next(it), next(it)) if has_act else (None, None)
    own, right_sum, left_sum = next(it), next(it), next(it)
    send_r, recv_r, send_l, recv_l = next(it), next(it), next(it), next(it)
    acc = next(it) if has_act else None

    chunks, width = up_v.shape[0], up_v.shape[2]
    streams = own.shape[0]
    me = lax.axis_index("dp")
    not_first, not_last = me > 0, me < n - 1

    def up_copy(c):
        cols = pl.ds(pl.multiple_of(c * width, width), width)
        return pltpu.make_async_copy(up_hbm.at[:, cols], up_v.at[c], up_sem.at[c])

    def down_copy(c):
        slots = down_v.shape[0]
        rows = pl.ds(pl.multiple_of(c * width, width), width)
        slot = lax.rem(c, slots)
        return pltpu.make_async_copy(down_hbm.at[rows, :], down_v.at[slot], down_sem.at[slot])

    def right_copy(s, c):
        return pltpu.make_async_remote_copy(
            right_sum.at[s, c], right_sum.at[s, c], send_r.at[s, c], recv_r.at[s, c],
            device_id={"dp": jnp.minimum(me + 1, n - 1)}, device_id_type=MESH)

    def left_copy(s, c):
        return pltpu.make_async_remote_copy(
            left_sum.at[s, c], left_sum.at[s, c], send_l.at[s, c], recv_l.at[s, c],
            device_id={"dp": jnp.maximum(me - 1, 0)}, device_id_type=MESH)

    if has_act:
        for c in range(min(down_v.shape[0], chunks)):
            down_copy(c).start()
    lax.fori_loop(0, chunks, lambda c, _: (up_copy(c).start(), 0)[1], 0)

    barrier = pltpu.get_barrier_semaphore()

    @pl.when(not_first)
    def _():
        pl.semaphore_signal(barrier, inc=1, device_id={"dp": me - 1}, device_id_type=MESH)

    @pl.when(not_last)
    def _():
        pl.semaphore_signal(barrier, inc=1, device_id={"dp": me + 1}, device_id_type=MESH)

    pl.semaphore_wait(barrier, jnp.where(not_first, 1, 0) + jnp.where(not_last, 1, 0))

    if has_act:
        acc[...] = jnp.zeros_like(acc)

    def forward(c, arrives, leaves, buf, copy):
        for s in range(streams):
            @pl.when(arrives)
            def _():
                copy(s, c).wait_recv()
                buf[s, c] = (buf[s, c].astype(jnp.float32) + own[s, c].astype(jnp.float32)).astype(jnp.bfloat16)

            @pl.when(jnp.logical_not(arrives))
            def _():
                buf[s, c] = own[s, c]

            @pl.when(leaves)
            def _():
                copy(s, c).start()

    def whole(s, c):
        return (right_sum[s, c].astype(jnp.float32) + left_sum[s, c].astype(jnp.float32)
                - own[s, c].astype(jnp.float32))

    def step(t, carry):
        @pl.when(t < chunks)
        def _():
            up_copy(t).wait()
            if has_pre:
                own[0, t] = jnp.dot(norm_ref[...], up_v[t], preferred_element_type=jnp.float32).astype(jnp.bfloat16)
            if has_act:
                down_copy(t).wait()
                own[streams - 1, t] = lax.dot_general(
                    inc_ref[...], down_v[lax.rem(t, down_v.shape[0])], (((1,), (1,)), ((), ())),
                    preferred_element_type=jnp.float32).astype(jnp.bfloat16)

                @pl.when(t + down_v.shape[0] < chunks)
                def _():
                    down_copy(t + down_v.shape[0]).start()

        cr = t - 2 * me
        @pl.when(jnp.logical_and(cr >= 0, cr < chunks))
        def _():
            forward(cr, not_first, not_last, right_sum, right_copy)

        cl = t - 2 * (n - 1 - me)
        @pl.when(jnp.logical_and(cl >= 0, cl < chunks))
        def _():
            forward(cl, not_last, not_first, left_sum, left_copy)

        c = t - 2 * (n - 1)
        @pl.when(c >= 0)
        def _():
            cols = pl.ds(pl.multiple_of(c * width, width), width)
            if has_pre:
                pre = whole(0, c)
                cdf = 0.5 * (1.0 + lax.erf(pre * inv_root_two))
                slope = cdf + pre * jnp.exp(-0.5 * pre * pre) * inv_root_two_pi
                act_ref[:, cols] = (pre * cdf).astype(jnp.bfloat16)
                if kind == "value":
                    slope_out[:, cols] = slope
            else:
                slope = slope_ref[:, cols]
            if has_act:
                grad = (whole(streams - 1, c) * slope).astype(jnp.bfloat16)
                pg_ref[:, cols] = grad
                acc[...] += lax.dot_general(grad, up_v[c], (((1,), (1,)), ((), ())),
                                            preferred_element_type=jnp.float32)
        return carry

    lax.fori_loop(0, chunks + 2 * (n - 1), step, 0)

    if has_act:
        ng_ref[...] = acc[...].astype(jnp.bfloat16)

    def drain(c, carry):
        for s in range(streams):
            @pl.when(not_last)
            def _():
                right_copy(s, c).wait_send()

            @pl.when(not_first)
            def _():
                left_copy(s, c).wait_send()
        return carry

    lax.fori_loop(0, chunks, drain, 0)


def relay(kind, collective_id, lhs, up, down=None):
    n = lax.axis_size("dp")
    tokens = lhs[0].shape[0]
    features, hidden = up.shape
    width = 256
    chunks = hidden // width
    has_pre, has_act = kind != "grad", kind != "value"
    streams = 2 if kind == "both" else 1
    vmem = pl.BlockSpec(memory_space=pltpu.VMEM)
    hbm = pl.BlockSpec(memory_space=pl.ANY)
    wide = jax.ShapeDtypeStruct((tokens, hidden), jnp.bfloat16)
    outs = []
    if has_pre:
        outs.append(wide)
    if kind == "value":
        outs.append(jax.ShapeDtypeStruct((tokens, hidden), jnp.float32))
    if has_act:
        outs += [wide, jax.ShapeDtypeStruct((tokens, features), jnp.bfloat16)]
    sems = pltpu.SemaphoreType.DMA
    scratch = [pltpu.VMEM((chunks, features, width), jnp.bfloat16), sems((chunks,))]
    if has_act:
        scratch += [pltpu.VMEM((4, width, features), jnp.bfloat16), sems((4,))]
    scratch += [pltpu.VMEM((streams, chunks, tokens, width), jnp.bfloat16)] * 3
    scratch += [sems((streams, chunks))] * 4
    if has_act:
        scratch.append(pltpu.VMEM((tokens, features), jnp.float32))
    weights = [up] + ([down] if has_act else [])
    products = (1 if has_pre else 0) + (2 if has_act else 0)
    return pl.pallas_call(
        functools.partial(relay_kernel, kind, n),
        out_shape=outs,
        in_specs=[vmem] * len(lhs) + [hbm] * len(weights),
        out_specs=[vmem] * len(outs),
        scratch_shapes=scratch,
        compiler_params=pltpu.CompilerParams(
            collective_id=collective_id, has_side_effects=True,
            vmem_limit_bytes=52 * 1024 * 1024),
        cost_estimate=pl.CostEstimate(
            flops=2 * tokens * features * hidden * products,
            bytes_accessed=streams * 160 * 1024 * 1024, transcendentals=0),
        name="relay_" + kind,
    )(*lhs, *weights)


def finish(partial_gradient, centered_input, inverse_deviation, scale_gain, local_rows):
    normalized_gradient = lax.psum_scatter(
        partial_gradient, "tensor", scatter_dimension=0, tiled=True).astype(jnp.float32)
    gain_product = jnp.sum(normalized_gradient * centered_input, axis=0)
    bias_term = jnp.sum(normalized_gradient, axis=0)
    centered_gradient = normalized_gradient * scale_gain
    centered_total, centered_cross = lax.psum(
        (
            jnp.sum(centered_gradient, axis=1, keepdims=True),
            jnp.sum(centered_gradient * centered_input, axis=1, keepdims=True),
        ),
        "dp",
    )
    final_output = local_rows.astype(jnp.float32) + inverse_deviation * (
        centered_gradient
        - centered_total / MODEL_WIDTH
        - centered_input * (centered_cross / MODEL_WIDTH)
    )
    return final_output.astype(jnp.bfloat16), gain_product, bias_term


def gather_rows(block):
    return lax.all_gather(block, "tensor", axis=0, tiled=True)


def body(layer_input, ready_grad, late_grad, norm_gain, norm_bias, up_weight, down_weight):
    early = lax.axis_index("section") == 0
    scale_gain = norm_gain[0]
    shift_bias = norm_bias[0]
    weight_up = up_weight[0]
    weight_down = down_weight[0]
    ready_whole = gather_rows(ready_grad[0])
    inputs_float = layer_input[0].astype(jnp.float32)
    row_total, row_squares = lax.psum(
        (
            jnp.sum(inputs_float, axis=2, keepdims=True),
            jnp.sum(inputs_float * inputs_float, axis=2, keepdims=True),
        ),
        "dp",
    )
    row_mean = row_total / MODEL_WIDTH
    variance = row_squares / MODEL_WIDTH - row_mean * row_mean
    inverse_deviation = lax.rsqrt(variance + epsilon)
    centered_input = (inputs_float - row_mean) * inverse_deviation
    normalized = (centered_input * scale_gain + shift_bias).astype(jnp.bfloat16)
    normed_first = gather_rows(normalized[0])
    act_first, pre_grad_first, partial_first = relay(
        "both", 1, [normed_first, ready_whole], weight_up, weight_down)
    normed_second = gather_rows(normalized[1])
    act_second, slope_second = relay("value", 2, [normed_second], weight_up)
    first_out, first_gain, first_bias = finish(
        partial_first, centered_input[0], inverse_deviation[0], scale_gain, ready_grad[0])

    arrived = lax.ppermute(first_out, "section", [(1, 0)])
    second_rows = jnp.where(early, arrived, late_grad)
    second_incoming = gather_rows(second_rows)
    pre_grad_second, partial_second = relay(
        "grad", 3, [second_incoming, slope_second], weight_up, weight_down)
    second_out, second_gain, second_bias = finish(
        partial_second, centered_input[1], inverse_deviation[1], scale_gain, second_rows)

    scale = 1.0 / math.sqrt(2 * second_incoming.shape[0])

    def weight_grad(left, right):
        return (lax.dot_general(
            jnp.concatenate(left), jnp.concatenate(right), (((0,), (0,)), ((), ())),
            preferred_element_type=jnp.float32) * scale).astype(jnp.bfloat16)

    down_part = weight_grad([act_first, act_second], [ready_whole, second_incoming])
    up_part = weight_grad([normed_first, normed_second], [pre_grad_first, pre_grad_second])
    gain_sum, bias_sum = lax.psum((first_gain + second_gain, first_bias + second_bias), "tensor")
    results = jnp.stack([first_out, second_out])
    return (
        results[None],
        up_part[None],
        down_part[None],
        (gain_sum * scale)[None],
        (bias_sum * scale)[None],
    )


def solution(mesh):
    in_specs = (
        P("section", None, "tensor", "dp"),
        P("section", "tensor", "dp"),
        P("tensor", "dp"),
        P("section", "dp"),
        P("section", "dp"),
        P("section", "dp", "tensor"),
        P("section", "tensor", "dp"),
    )
    out_specs = (
        P("section", None, "tensor", "dp"),
        P("section", "dp", "tensor"),
        P("section", "tensor", "dp"),
        P("section", "dp"),
        P("section", "dp"),
    )
    return jax.shard_map(body, mesh=mesh, in_specs=in_specs, out_specs=out_specs, check_vma=False)
```

time: 602 us -> 398 us (0.66); the launches traced: 595 us -> 397 us
  waiting for transfers between devices: 366 us -> 51.6 us
  Pallas kernels: 0 us -> 244 us
  matrix products: 146 us -> 27.6 us
  other arithmetic: 19.2 us -> 11.4 us
    pallas_call x0 -> x3, Pallas kernels: none -> 244 us  [relay(): pl.pallas_call(functools.partial(relay_kernel, kind, n), out_shape=outs,...]
    reduce_scatter x6 -> x2, waiting for transfers between devices: 177 us -> 21.6 us  [finish(): lax.psum_scatter(partial_gradient, 'tensor', scatter_dimension=0, tiled=T...]
    all_gather x9 -> x4, waiting for transfers between devices: 177 us -> 21.8 us  [gather_rows(): return lax.all_gather(block, 'tensor', axis=0, tiled=True)]
    dot_general x10 -> x2, matrix products: 146 us -> 27.6 us  [weight_grad(): lax.dot_general(jnp.concatenate(left), jnp.concatenate(right), (((0,), (0...]
    convert_element_type x4 -> x2, other arithmetic: 9.42 us -> 2.59 us  [the longest x1 1.45 us: body(): normalized = (centered_input * scale_gain + shift_bias).astype(jnp.bfloat16)]
  transfers between devices with their start and end apart: 16 -> 7, of which waited for: 16 -> 4; matrix products, arithmetic and copies ran while one was open for 23% -> 9% of each run, Pallas kernels for 0% -> 15%
where the time goes in v1:
time: 398 us; the launch traced here: 397 us
  Pallas kernels  244 us (61%)
  waiting for transfers between devices  51.6 us (13%)
  blocking collectives  44.9 us (11%)
  matrix products  27.6 us (7%)
  between operations  14.3 us (4%)
  other arithmetic  11.4 us (3%)
    pallas_call x3, Pallas kernels, relay(): pl.pallas_call(functools.partial(relay_kernel, kind, n), out_shape=outs,...  244 us
    dot_general x2, matrix products, weight_grad(): lax.dot_general(jnp.concatenate(left), jnp.concatenate(right), (((0,), (0...  27.6 us
    all_gather x4, waiting for transfers between devices, gather_rows(): return lax.all_gather(block, 'tensor', axis=0, tiled=True)  21.8 us
    reduce_scatter x2, waiting for transfers between devices, finish(): lax.psum_scatter(partial_gradient, 'tensor', scatter_dimension=0, tiled=T...  21.6 us
    psum x2, blocking collectives, finish(): lax.psum((jnp.sum(centered_gradient, axis=1, keepdims=True), jnp.sum(cent...  21.4 us
    psum x1, blocking collectives, body(): lax.psum((jnp.sum(inputs_float, axis=2, keepdims=True), jnp.sum(inputs_fl...  13.4 us
    psum x1, blocking collectives, body(): lax.psum((first_gain + second_gain, first_bias + second_bias), 'tensor')  10.1 us
  transfers between devices with their start and end apart: 7, of which 4 were waited for; matrix products, arithmetic and copies ran while one was open for 9% of the time, Pallas kernels for 15%

profile of v1, /device:TPU:0, one launch (start us, length us, event | category | flops | bytes accessed | tf_op | source)
XLA Modules:
  0.0 397.3 jit_solution(16120736739993666396)
XLA Ops:
  7.9 1.2 convert_reduce_fusion
  9.1 1.2 fusion.16
  10.4 13.4 %all-reduce.3 = (f32[2,64,1]{1,0,2:T(2,128)S(1)}, f32[2,64,1]{1,0,2:T(2,128)S(1)}) all-reduce(f32[2,64,1]{1,0,2:T(2,128)S(1)} %bitcast.90, f32[2,64,1]{1,0,2:T(2,128)S(1)} %bitcast.89), channel_id=1, replica_groups=mesh['section'=2,'dp'=4,'tensor'=4] {'dp'}, use_global_device_ids=true, to_apply=%region_1.0 | all-reduce | flops 256 | bytes 2048 | tf_op jit(solution)/shard_map/psum | solution.py:242
  23.8 1.5 add_convert_fusion
  25.3 0.8 fusion.39
  26.2 2.8 all-gather.12.cloned.1.call-done
  29.0 18.9 %all-gather.10.cloned.1.call-done = bf16[1,256,2048]{2,1,0:T(8,128)(2,1)} async-done(((bf16[1,64,2048]{2,1,0:T(8,128)(2,1)}), bf16[1,256,2048]{2,1,0:T(8,128)(2,1)}) %all-gather.10.cloned.1.call-update) | async-done | bytes 1048592 | tf_op jit(solution)/shard_map/all_gather | solution.py:231
  47.9 120.6 %relay_both.1 = (bf16[256,4096]{1,0:T(8,128)(2,1)}, bf16[256,4096]{1,0:T(8,128)(2,1)}, bf16[256,2048]{1,0:T(8,128)(2,1)}) custom-call(bf16[256,2048]{1,0:T(8,128)(2,1)} %bitcast.97, bf16[256,2048]{1,0:T(8,128)(2,1)} %bitcast.95, bf16[2048,4096]{1,0:T(8,128)(2,1)} %bitcast.74, bf16[4096,2048]{1,0:T(8,128)(2,1)} %bitcast.77), custom_call_target="tpu_custom_call" | custom-call | flops 12884901888 | bytes 335544320 | tf_op jit(solution)/shard_map/relay_both/pallas_call | solution.py:193
  169.1 21.6 %reduce-scatter.3.cloned.1.call-done = bf16[64,2048]{1,0:T(8,128)(2,1)} async-done(((bf16[256,2048]{1,0:T(8,128)(2,1)}), bf16[64,2048]{1,0:T(8,128)(2,1)}) %reduce-scatter.3.cloned.1.call-update) | async-done | bytes 262160 | tf_op jit(solution)/shard_map/reduce_scatter | solution.py:210
  190.8 1.2 fusion.34
  192.0 11.7 %all-reduce.2 = (f32[64,1]{0,1:T(1,128)S(1)}, f32[64,1]{0,1:T(1,128)S(1)}) all-reduce(f32[64,1]{0,1:T(1,128)S(1)} %bitcast.91, f32[64,1]{0,1:T(1,128)S(1)} %bitcast.92), channel_id=1, replica_groups=mesh['section'=2,'dp'=4,'tensor'=4] {'dp'}, use_global_device_ids=true, to_apply=%region_8.0 | all-reduce | flops 128 | bytes 1024 | tf_op jit(solution)/shard_map/psum | solution.py:215
  203.7 1.1 fusion.32
  204.9 1.3 collective-permute-start
  206.2 7.0 %collective-permute-done = bf16[64,2048]{1,0:T(8,128)(2,1)S(1)} collective-permute-done((bf16[64,2048]{1,0:T(8,128)(2,1)S(1)}, bf16[64,2048]{1,0:T(8,128)(2,1)S(1)}, u32[]{:S(2)}, u32[]{:S(2)}) %collective-permute-start) | collective-permute-done | bytes 262176 | tf_op jit(solution)/shard_map/ppermute | solution.py:262
  214.0 1.2 copy-done
  215.2 59.9 %relay_value.1 = (bf16[256,4096]{1,0:T(8,128)(2,1)}, f32[256,4096]{1,0:T(8,128)}) custom-call(bf16[256,2048]{1,0:T(8,128)(2,1)S(1)} %bitcast.72, bf16[2048,4096]{1,0:T(8,128)(2,1)} %bitcast.75), custom_call_target="tpu_custom_call" | custom-call | flops 4294967296 | bytes 167772160 | tf_op jit(solution)/shard_map/relay_value/pallas_call | solution.py:193
  275.2 63.3 %relay_grad.1 = (bf16[256,4096]{1,0:T(8,128)(2,1)}, bf16[256,2048]{1,0:T(8,128)(2,1)}) custom-call(bf16[256,2048]{1,0:T(8,128)(2,1)} %all-gather.8.cloned.1.call-done.refs_0_, f32[256,4096]{1,0:T(8,128)} %get-tuple-element.13.refs_1_, bf16[2048,4096]{1,0:T(8,128)(2,1)} %bitcast.76, bf16[4096,2048]{1,0:T(8,128)(2,1)} %bitcast.78), custom_call_target="tpu_custom_call" | custom-call | flops 8589934592 | bytes 167772160 | tf_op jit(solution)/shard_map/relay_grad/pallas_call | solution.py:193
  338.6 15.0 %fusion = bf16[1,2048,4096]{2,1,0:T(8,128)(2,1)} fusion(bf16[256,4096]{1,0:T(8,128)(2,1)} %get-tuple-element.16, bf16[256,4096]{1,0:T(8,128)(2,1)} %get-tuple-element.15, bf16[256,2048]{1,0:T(8,128)(2,1)S(1)} %bitcast.73, bf16[256,2048]{1,0:T(8,128)(2,1)S(1)} %bitcast.98), kind=kOutput, calls=%fused_computation.2 | convolution fusion | flops 8619294720 | bytes 23068672 | tf_op jit(solution)/shard_map/dot_general | solution.py:273
  353.6 12.6 %fusion.1 = bf16[1,4096,2048]{2,1,0:T(8,128)(2,1)} fusion(bf16[256,4096]{1,0:T(8,128)(2,1)S(1)} %copy-done.7, bf16[256,4096]{1,0:T(8,128)(2,1)S(1)} %copy-done.10, bf16[256,2048]{1,0:T(8,128)(2,1)S(1)} %copy-done.3, bf16[256,2048]{1,0:T(8,128)(2,1)S(1)} %bitcast.96), kind=kOutput, calls=%fused_computation.3 | convolution fusion | flops 8619294720 | bytes 23068672 | tf_op jit(solution)/shard_map/dot_general | solution.py:273
  366.2 1.2 fusion.35
  367.4 9.7 %all-reduce.1 = (f32[64,1]{0,1:T(1,128)S(1)}, f32[64,1]{0,1:T(1,128)S(1)}) all-reduce(f32[64,1]{0,1:T(1,128)S(1)} %bitcast.93, f32[64,1]{0,1:T(1,128)S(1)} %bitcast.94), channel_id=1, replica_groups=mesh['section'=2,'dp'=4,'tensor'=4] {'dp'}, use_global_device_ids=true, to_apply=%region_13.14 | all-reduce | flops 128 | bytes 1024 | tf_op jit(solution)/shard_map/psum | solution.py:215
  377.1 10.1 %all-reduce = (f32[2048]{0:T(1024)S(1)}, f32[2048]{0:T(1024)S(1)}) all-reduce(f32[2048]{0:T(1024)S(1)} %add.55, f32[2048]{0:T(1024)S(1)} %add.56), channel_id=1, replica_groups=mesh['section'=2,'dp'=4,'tensor'=4] {'tensor'}, use_global_device_ids=true, to_apply=%region_16.17 | all-reduce | flops 4096 | bytes 32768 | tf_op jit(solution)/shard_map/psum | solution.py:279
  388.4 1.1 fusion.36
  389.6 0.8 maximum_bitcast_fusion
  (46 shorter events, 3.6 us)
Async XLA Ops:
  7.2 21.8 %all-gather.12.cloned.1.call-start = ((), (), s32[]{:S(2)}) async-start(), calls=%async_computation.6 | async-start | bytes 1310720 | tf_op jit(solution)/shard_map/all_gather | solution.py:231
  7.9 40.0 %all-gather.10.cloned.1.call-start = ((), (), s32[]{:S(2)}) async-start(), calls=%async_computation.5 | async-start | bytes 1310720 | tf_op jit(solution)/shard_map/all_gather | solution.py:231
  26.1 164.6 %reduce-scatter.3.cloned.1.call-start = ((), (), s32[]{:S(2)}) async-start(), calls=%async_computation.2 | async-start | bytes 1310720 | tf_op jit(solution)/shard_map/reduce_scatter | solution.py:210
  47.9 142.9 %copy-start.6 = (f32[1,2048]{1,0:T(1,128)S(1)}, f32[1,2048]{1,0:T(1,128)}, u32[]{:S(2)}) copy-start(f32[1,2048]{1,0:T(1,128)} %param.10) | copy-start | bytes 24580
  47.9 155.8 %copy-start.4 = (bf16[1,64,2048]{2,1,0:T(8,128)(2,1)S(1)}, bf16[1,64,2048]{2,1,0:T(8,128)(2,1)}, u32[]{:S(2)}) copy-start(bf16[1,64,2048]{2,1,0:T(8,128)(2,1)} %param.8) | copy-start | bytes 786436
  47.9 165.2 %copy-start.5 = (bf16[64,2048]{1,0:T(8,128)(2,1)S(1)}, bf16[64,2048]{1,0:T(8,128)(2,1)}, u32[]{:S(2)}) copy-start(bf16[64,2048]{1,0:T(8,128)(2,1)} %param.9) | copy-start | bytes 786436
  168.5 45.5 %all-gather.14.cloned.1.call-start = ((), (), s32[]{:S(2)}) async-start(), calls=%async_computation.7 | async-start | bytes 1310720 | tf_op jit(solution)/shard_map/all_gather | solution.py:231
  169.1 106.1 %all-gather.8.cloned.1.call-start = ((), (), s32[]{:S(2)}) async-start(), calls=%async_computation.3 | async-start | bytes 1310720 | tf_op jit(solution)/shard_map/all_gather | solution.py:231
  204.9 8.3 %collective-permute-start = (bf16[64,2048]{1,0:T(8,128)(2,1)S(1)}, bf16[64,2048]{1,0:T(8,128)(2,1)S(1)}, u32[]{:S(2)}, u32[]{:S(2)}) collective-permute-start(bf16[64,2048]{1,0:T(8,128)(2,1)S(1)} %fusion.32), channel_id=1, source_target_pairs={{16,0},{17,1},{18,2},{19,3},{20,4},{21,5},{22,6},{23,7},{24,8},{25... | collective-permute-start | bytes 786440 | tf_op jit(solution)/shard_map/ppermute | solution.py:262
  213.9 152.3 %reduce-scatter.5.cloned.1.call-start = ((), (), s32[]{:S(2)}) async-start(), calls=%async_computation.4 | async-start | bytes 1310720 | tf_op jit(solution)/shard_map/reduce_scatter | solution.py:210
  214.0 1.2 copy-start
  275.2 63.3 %copy-start.1 = (bf16[1,256,2048]{2,1,0:T(8,128)(2,1)S(1)}, bf16[1,256,2048]{2,1,0:T(8,128)(2,1)}, u32[]{:S(2)}) copy-start(bf16[1,256,2048]{2,1,0:T(8,128)(2,1)} %all-gather.14.cloned.1.call-done) | copy-start | bytes 3145732
  275.2 63.3 %copy-start.9 = (bf16[1,256,2048]{2,1,0:T(8,128)(2,1)S(1)}, bf16[1,256,2048]{2,1,0:T(8,128)(2,1)}, u32[]{:S(2)}) copy-start(bf16[1,256,2048]{2,1,0:T(8,128)(2,1)} %all-gather.10.cloned.1.call-done) | copy-start | bytes 3145732
  338.5 15.0 %copy-start.3 = (bf16[256,2048]{1,0:T(8,128)(2,1)S(1)}, bf16[256,2048]{1,0:T(8,128)(2,1)}, u32[]{:S(2)}) copy-start(bf16[256,2048]{1,0:T(8,128)(2,1)} %all-gather.8.cloned.1.call-done.refs_0_) | copy-start | bytes 3145732
  338.5 15.0 %copy-start.7 = (bf16[256,4096]{1,0:T(8,128)(2,1)S(1)}, bf16[256,4096]{1,0:T(8,128)(2,1)}, u32[]{:S(2)}) copy-start(bf16[256,4096]{1,0:T(8,128)(2,1)} %get-tuple-element.18) | copy-start | bytes 6291460
  338.5 15.0 %copy-start.8 = (bf16[1,256,2048]{2,1,0:T(8,128)(2,1)S(1)}, bf16[1,256,2048]{2,1,0:T(8,128)(2,1)}, u32[]{:S(2)}) copy-start(bf16[1,256,2048]{2,1,0:T(8,128)(2,1)} %all-gather.12.cloned.1.call-done) | copy-start | bytes 3145732
  338.5 15.0 %copy-start.10 = (bf16[256,4096]{1,0:T(8,128)(2,1)S(1)}, bf16[256,4096]{1,0:T(8,128)(2,1)}, u32[]{:S(2)}) copy-start(bf16[256,4096]{1,0:T(8,128)(2,1)} %get-tuple-element.17) | copy-start | bytes 6291460
  353.5 34.9 %copy-start.2 = (bf16[64,2048]{1,0:T(8,128)(2,1)S(1)}, bf16[64,2048]{1,0:T(8,128)(2,1)}, u32[]{:S(2)}) copy-start(bf16[64,2048]{1,0:T(8,128)(2,1)} %broadcast_select_fusion) | copy-start | bytes 786436
Sparse Core Ops, SparseCore 0:
  9.6 19.4 all-gather.11
  31.1 16.7 all-gather.9
  168.6 22.1 reduce-scatter.2
  192.8 16.7 all-gather.13
  214.0 13.7 all-gather.7
  338.6 23.5 reduce-scatter.4

commit v2 on v1

--- a/solution.py
+++ b/solution.py
@@ -16,12 +16,12 @@
 inv_root_two_pi = 0.3989422804014327
 
 
-def relay_kernel(kind, n, *refs):
+def relay_kernel(kind, n, first, *refs):
     has_pre, has_act = kind != "grad", kind != "value"
     it = iter(refs)
     norm_ref = next(it) if has_pre else None
     inc_ref = next(it) if has_act else None
-    slope_ref = next(it) if kind == "grad" else None
+    slope_refs = (next(it), next(it)) if kind == "grad" else None
     up_hbm = next(it)
     down_hbm = next(it) if has_act else None
     act_ref = next(it) if has_pre else None
@@ -32,30 +32,33 @@
     own, right_sum, left_sum = next(it), next(it), next(it)
     send_r, recv_r, send_l, recv_l = next(it), next(it), next(it), next(it)
     acc = next(it) if has_act else None
+    slope_v = next(it) if kind == "grad" else None
 
     chunks, width = up_v.shape[0], up_v.shape[2]
-    streams = own.shape[0]
+    streams, parts, rows = own.shape[0], own.shape[2], own.shape[3]
     me = lax.axis_index("dp")
     not_first, not_last = me > 0, me < n - 1
 
     def up_copy(c):
-        cols = pl.ds(pl.multiple_of(c * width, width), width)
+        cols = pl.ds(pl.multiple_of((first + c) * width, width), width)
         return pltpu.make_async_copy(up_hbm.at[:, cols], up_v.at[c], up_sem.at[c])
 
     def down_copy(c):
         slots = down_v.shape[0]
-        rows = pl.ds(pl.multiple_of(c * width, width), width)
+        span = pl.ds(pl.multiple_of(c * width, width), width)
         slot = lax.rem(c, slots)
-        return pltpu.make_async_copy(down_hbm.at[rows, :], down_v.at[slot], down_sem.at[slot])
-
-    def right_copy(s, c):
+        return pltpu.make_async_copy(down_hbm.at[span, :], down_v.at[slot], down_sem.at[slot])
+
+    def right_copy(s, c, h):
+        block = right_sum.at[s, c, h]
         return pltpu.make_async_remote_copy(
-            right_sum.at[s, c], right_sum.at[s, c], send_r.at[s, c], recv_r.at[s, c],
+            block, block, send_r.at[s, c, h], recv_r.at[s, c, h],
             device_id={"dp": jnp.minimum(me + 1, n - 1)}, device_id_type=MESH)
 
-    def left_copy(s, c):
+    def left_copy(s, c, h):
+        block = left_sum.at[s, c, h]
         return pltpu.make_async_remote_copy(
-            left_sum.at[s, c], left_sum.at[s, c], send_l.at[s, c], recv_l.at[s, c],
+            block, block, send_l.at[s, c, h], recv_l.at[s, c, h],
             device_id={"dp": jnp.maximum(me - 1, 0)}, device_id_type=MESH)
 
     if has_act:
@@ -78,50 +81,55 @@
     if has_act:
         acc[...] = jnp.zeros_like(acc)
 
-    def forward(c, arrives, leaves, buf, copy):
-        for s in range(streams):
-            @pl.when(arrives)
-            def _():
-                copy(s, c).wait_recv()
-                buf[s, c] = (buf[s, c].astype(jnp.float32) + own[s, c].astype(jnp.float32)).astype(jnp.bfloat16)
-
-            @pl.when(jnp.logical_not(arrives))
-            def _():
-                buf[s, c] = own[s, c]
-
-            @pl.when(leaves)
-            def _():
-                copy(s, c).start()
+    def forward(s, c, h, arrives, leaves, buf, copy):
+        @pl.when(arrives)
+        def _():
+            copy(s, c, h).wait_recv()
+            buf[s, c, h] = (buf[s, c, h].astype(jnp.float32) + own[s, c, h].astype(jnp.float32)).astype(jnp.bfloat16)
+
+        @pl.when(jnp.logical_not(arrives))
+        def _():
+            buf[s, c, h] = own[s, c, h]
+
+        @pl.when(leaves)
+        def _():
+            copy(s, c, h).start()
 
     def whole(s, c):
-        return (right_sum[s, c].astype(jnp.float32) + left_sum[s, c].astype(jnp.float32)
-                - own[s, c].astype(jnp.float32))
+        total = (right_sum[s, c].astype(jnp.float32) + left_sum[s, c].astype(jnp.float32)
+                 - own[s, c].astype(jnp.float32))
+        return total.reshape(parts * rows, width)
+
+    def keep(s, c, product):
+        own[s, c] = product.astype(jnp.bfloat16).reshape(parts, rows, width)
 
     def step(t, carry):
         @pl.when(t < chunks)
         def _():
             up_copy(t).wait()
             if has_pre:
-                own[0, t] = jnp.dot(norm_ref[...], up_v[t], preferred_element_type=jnp.float32).astype(jnp.bfloat16)
+                keep(0, t, jnp.dot(norm_ref[...], up_v[t], preferred_element_type=jnp.float32))
             if has_act:
                 down_copy(t).wait()
-                own[streams - 1, t] = lax.dot_general(
+                keep(streams - 1, t, lax.dot_general(
                     inc_ref[...], down_v[lax.rem(t, down_v.shape[0])], (((1,), (1,)), ((), ())),
-                    preferred_element_type=jnp.float32).astype(jnp.bfloat16)
+                    preferred_element_type=jnp.float32))
 
                 @pl.when(t + down_v.shape[0] < chunks)
                 def _():
                     down_copy(t + down_v.shape[0]).start()
 
         cr = t - 2 * me
-        @pl.when(jnp.logical_and(cr >= 0, cr < chunks))
-        def _():
-            forward(cr, not_first, not_last, right_sum, right_copy)
-
         cl = t - 2 * (n - 1 - me)
-        @pl.when(jnp.logical_and(cl >= 0, cl < chunks))
-        def _():
-            forward(cl, not_last, not_first, left_sum, left_copy)
+        for h in range(parts):
+            for s in range(streams):
+                @pl.when(jnp.logical_and(cr >= 0, cr < chunks))
+                def _():
+                    forward(s, cr, h, not_first, not_last, right_sum, right_copy)
+
+                @pl.when(jnp.logical_and(cl >= 0, cl < chunks))
+                def _():
+                    forward(s, cl, h, not_last, not_first, left_sum, left_copy)
 
         c = t - 2 * (n - 1)
         @pl.when(c >= 0)
@@ -135,7 +143,14 @@
                 if kind == "value":
                     slope_out[:, cols] = slope
             else:
-                slope = slope_ref[:, cols]
+                half = chunks // 2
+                for side in range(2):
+                    @pl.when(c // half == side)
+                    def _():
+                        part = pl.ds(pl.multiple_of((c - side * half) * width, width), width)
+                        slope_v[...] = slope_refs[side][:, part]
+
+                slope = slope_v[...]
             if has_act:
                 grad = (whole(streams - 1, c) * slope).astype(jnp.bfloat16)
                 pg_ref[:, cols] = grad
@@ -150,23 +165,24 @@
 
     def drain(c, carry):
         for s in range(streams):
-            @pl.when(not_last)
-            def _():
-                right_copy(s, c).wait_send()
-
-            @pl.when(not_first)
-            def _():
-                left_copy(s, c).wait_send()
+            for h in range(parts):
+                @pl.when(not_last)
+                def _():
+                    right_copy(s, c, h).wait_send()
+
+                @pl.when(not_first)
+                def _():
+                    left_copy(s, c, h).wait_send()
         return carry
 
     lax.fori_loop(0, chunks, drain, 0)
 
 
-def relay(kind, collective_id, lhs, up, down=None):
+def relay(kind, collective_id, lhs, up, down=None, first=0, share=1):
     n = lax.axis_size("dp")
     tokens = lhs[0].shape[0]
-    features, hidden = up.shape
-    width = 256
+    features, hidden = up.shape[0], up.shape[1] // share
+    width, parts = 256, 2
     chunks = hidden // width
     has_pre, has_act = kind != "grad", kind != "value"
     streams = 2 if kind == "both" else 1
@@ -184,14 +200,16 @@
     scratch = [pltpu.VMEM((chunks, features, width), jnp.bfloat16), sems((chunks,))]
     if has_act:
         scratch += [pltpu.VMEM((4, width, features), jnp.bfloat16), sems((4,))]
-    scratch += [pltpu.VMEM((streams, chunks, tokens, width), jnp.bfloat16)] * 3
-    scratch += [sems((streams, chunks))] * 4
+    scratch += [pltpu.VMEM((streams, chunks, parts, tokens // parts, width), jnp.bfloat16)] * 3
+    scratch += [sems((streams, chunks, parts))] * 4
     if has_act:
         scratch.append(pltpu.VMEM((tokens, features), jnp.float32))
+    if kind == "grad":
+        scratch.append(pltpu.VMEM((tokens, width), jnp.float32))
     weights = [up] + ([down] if has_act else [])
     products = (1 if has_pre else 0) + (2 if has_act else 0)
     return pl.pallas_call(
-        functools.partial(relay_kernel, kind, n),
+        functools.partial(relay_kernel, kind, n, first * (hidden // width)),
         out_shape=outs,
         in_specs=[vmem] * len(lhs) + [hbm] * len(weights),
         out_specs=[vmem] * len(outs),
@@ -201,14 +219,17 @@
             vmem_limit_bytes=52 * 1024 * 1024),
         cost_estimate=pl.CostEstimate(
             flops=2 * tokens * features * hidden * products,
-            bytes_accessed=streams * 160 * 1024 * 1024, transcendentals=0),
-        name="relay_" + kind,
+            bytes_accessed=streams * 160 * 1024 * 1024 // share, transcendentals=0),
+        name="relay_%s_%d" % (kind, first),
     )(*lhs, *weights)
 
 
-def finish(partial_gradient, centered_input, inverse_deviation, scale_gain, local_rows):
-    normalized_gradient = lax.psum_scatter(
-        partial_gradient, "tensor", scatter_dimension=0, tiled=True).astype(jnp.float32)
+def scatter_rows(partial_gradient):
+    return lax.psum_scatter(partial_gradient, "tensor", scatter_dimension=0, tiled=True)
+
+
+def finish(scattered, centered_input, inverse_deviation, scale_gain, local_rows):
+    normalized_gradient = scattered.astype(jnp.float32)
     gain_product = jnp.sum(normalized_gradient * centered_input, axis=0)
     bias_term = jnp.sum(normalized_gradient, axis=0)
     centered_gradient = normalized_gradient * scale_gain
@@ -255,17 +276,23 @@
     act_first, pre_grad_first, partial_first = relay(
         "both", 1, [normed_first, ready_whole], weight_up, weight_down)
     normed_second = gather_rows(normalized[1])
-    act_second, slope_second = relay("value", 2, [normed_second], weight_up)
+    normed_second, partial_first = lax.optimization_barrier((normed_second, partial_first))
+    scattered = scatter_rows(partial_first)
+    act_low, slope_low = relay("value", 2, [normed_second], weight_up, first=0, share=2)
+    scattered, act_low = lax.optimization_barrier((scattered, act_low))
     first_out, first_gain, first_bias = finish(
-        partial_first, centered_input[0], inverse_deviation[0], scale_gain, ready_grad[0])
+        scattered, centered_input[0], inverse_deviation[0], scale_gain, ready_grad[0])
 
     arrived = lax.ppermute(first_out, "section", [(1, 0)])
     second_rows = jnp.where(early, arrived, late_grad)
+    second_rows, normed_second = lax.optimization_barrier((second_rows, normed_second))
     second_incoming = gather_rows(second_rows)
+    act_high, slope_high = relay("value", 4, [normed_second], weight_up, first=1, share=2)
+    act_second = jnp.concatenate([act_low, act_high], axis=1)
     pre_grad_second, partial_second = relay(
-        "grad", 3, [second_incoming, slope_second], weight_up, weight_down)
+        "grad", 3, [second_incoming, slope_low, slope_high], weight_up, weight_down)
     second_out, second_gain, second_bias = finish(
-        partial_second, centered_input[1], inverse_deviation[1], scale_gain, second_rows)
+        scatter_rows(partial_second), centered_input[1], inverse_deviation[1], scale_gain, second_rows)
 
     scale = 1.0 / math.sqrt(2 * second_incoming.shape[0])
 
@@ -276,7 +303,8 @@
 
     down_part = weight_grad([act_first, act_second], [ready_whole, second_incoming])
     up_part = weight_grad([normed_first, normed_second], [pre_grad_first, pre_grad_second])
-    gain_sum, bias_sum = lax.psum((first_gain + second_gain, first_bias + second_bias), "tensor")
+    token_sums = jnp.stack([first_gain + second_gain, first_bias + second_bias])
+    gain_sum, bias_sum = jnp.sum(lax.all_gather(token_sums, "tensor", axis=0), axis=0)
     results = jnp.stack([first_out, second_out])
     return (
         results[None],

time: 398 us -> 373 us (0.937)
  waiting for transfers between devices: 51.6 us -> 29.4 us
  blocking collectives: 44.9 us -> 38.2 us
  Pallas kernels: 244 us -> 249 us
    reduce_scatter x2, waiting for transfers between devices: 21.6 us -> 0.02 us  [scatter_rows(): lax.psum_scatter(partial_gradient, 'tensor', scatter_dimension=0, tiled=T...]
    psum x1 -> x0, blocking collectives: 10.1 us -> none  [body(): lax.psum((first_gain + second_gain, first_bias + second_bias), 'tensor')]
    all_gather x0 -> x1, blocking collectives: none -> 5.25 us  [body(): lax.all_gather(token_sums, 'tensor', axis=0)]
    pallas_call x3 -> x4, Pallas kernels: 244 us -> 249 us  [relay(): pl.pallas_call(functools.partial(relay_kernel, kind, n, first * (hidden /...]
  transfers between devices with their start and end apart: 7 -> 7, of which waited for: 4 -> 3; matrix products, arithmetic and copies ran while one was open for 9% -> 9% of each run, Pallas kernels for 15% -> 51%
where the time goes in v2:
time: 373 us
  Pallas kernels  249 us (67%)
  blocking collectives  38.2 us (10%)
  waiting for transfers between devices  29.4 us (8%)
  matrix products  29.1 us (8%)
  between operations  14.3 us (4%)
  other arithmetic  10.9 us (3%)
    pallas_call x4, Pallas kernels, relay(): pl.pallas_call(functools.partial(relay_kernel, kind, n, first * (hidden /...  249 us
    dot_general x2, matrix products, weight_grad(): lax.dot_general(jnp.concatenate(left), jnp.concatenate(right), (((0,), (0...  29.1 us
    all_gather x4, waiting for transfers between devices, gather_rows(): return lax.all_gather(block, 'tensor', axis=0, tiled=True)  21 us
    psum x2, blocking collectives, finish(): lax.psum((jnp.sum(centered_gradient, axis=1, keepdims=True), jnp.sum(cent...  19.5 us
    psum x1, blocking collectives, body(): lax.psum((jnp.sum(inputs_float, axis=2, keepdims=True), jnp.sum(inputs_fl...  13.4 us
  transfers between devices with their start and end apart: 7, of which 3 were waited for; matrix products, arithmetic and copies ran while one was open for 9% of the time, Pallas kernels for 51%

profile of v2, /device:TPU:0, one launch (start us, length us, event | category | flops | bytes accessed | tf_op | source)
XLA Modules:
  0.0 372.9 jit_solution(10525562269543363826)
XLA Ops:
  7.9 1.2 convert_reduce_fusion
  9.1 1.2 fusion.18
  10.4 13.4 %all-reduce.2 = (f32[2,64,1]{1,0,2:T(2,128)S(1)}, f32[2,64,1]{1,0,2:T(2,128)S(1)}) all-reduce(f32[2,64,1]{1,0,2:T(2,128)S(1)} %bitcast.94, f32[2,64,1]{1,0,2:T(2,128)S(1)} %bitcast.93), channel_id=1, replica_groups=mesh['section'=2,'dp'=4,'tensor'=4] {'dp'}, use_global_device_ids=true, to_apply=%region_1.0 | all-reduce | flops 256 | bytes 2048 | tf_op jit(solution)/shard_map/psum | solution.py:263
  23.8 1.5 add_convert_fusion
  25.3 0.8 fusion.41
  26.9 2.1 all-gather.16.cloned.1.call-done
  29.0 18.9 %all-gather.14.cloned.1.call-done = bf16[1,256,2048]{2,1,0:T(8,128)(2,1)} async-done(((bf16[1,64,2048]{2,1,0:T(8,128)(2,1)}), bf16[1,256,2048]{2,1,0:T(8,128)(2,1)}) %all-gather.14.cloned.1.call-update) | async-done | bytes 1048592 | tf_op jit(solution)/shard_map/all_gather | solution.py:252
  47.9 118.1 %relay_both_0.1 = (bf16[256,4096]{1,0:T(8,128)(2,1)}, bf16[256,4096]{1,0:T(8,128)(2,1)}, bf16[256,2048]{1,0:T(8,128)(2,1)}) custom-call(bf16[256,2048]{1,0:T(8,128)(2,1)} %bitcast.101, bf16[256,2048]{1,0:T(8,128)(2,1)} %bitcast.99, bf16[2048,4096]{1,0:T(8,128)(2,1)} %bitcast.74, bf16[4096,2048]{1,0:T(8,128)(2,1)} %bitcast.78), custom_call_target="tpu_custom_call" | custom-call | flops 12884901888 | bytes 335544320 | tf_op jit(solution)/shard_map/relay_both_0/pallas_call | solution.py:211
  166.2 38.4 %relay_value_0.1 = (bf16[256,2048]{1,0:T(8,128)(2,1)S(1)}, f32[256,2048]{1,0:T(8,128)}) custom-call(bf16[256,2048]{1,0:T(8,128)(2,1)} %bitcast.80, bf16[2048,4096]{1,0:T(8,128)(2,1)} %bitcast.75), custom_call_target="tpu_custom_call" | custom-call | flops 2147483648 | bytes 83886080 | tf_op jit(solution)/shard_map/relay_value_0/pallas_call | solution.py:211
  204.6 1.2 fusion.36
  205.8 9.7 %all-reduce.1 = (f32[64,1]{0,1:T(1,128)S(1)}, f32[64,1]{0,1:T(1,128)S(1)}) all-reduce(f32[64,1]{0,1:T(1,128)S(1)} %bitcast.95, f32[64,1]{0,1:T(1,128)S(1)} %bitcast.96), channel_id=1, replica_groups=mesh['section'=2,'dp'=4,'tensor'=4] {'dp'}, use_global_device_ids=true, to_apply=%region_8.0 | all-reduce | flops 128 | bytes 1024 | tf_op jit(solution)/shard_map/psum | solution.py:236
  215.5 1.1 fusion.34
  216.7 1.3 collective-permute-start
  218.0 7.0 %collective-permute-done = bf16[64,2048]{1,0:T(8,128)(2,1)S(1)} collective-permute-done((bf16[64,2048]{1,0:T(8,128)(2,1)S(1)}, bf16[64,2048]{1,0:T(8,128)(2,1)S(1)}, u32[]{:S(2)}, u32[]{:S(2)}) %collective-permute-start) | collective-permute-done | bytes 262176 | tf_op jit(solution)/shard_map/ppermute | solution.py:286
  224.9 0.7 broadcast_select_fusion
  225.7 33.4 %relay_value_1.1 = (bf16[256,2048]{1,0:T(8,128)(2,1)S(1)}, f32[256,2048]{1,0:T(8,128)}) custom-call(bf16[256,2048]{1,0:T(8,128)(2,1)} %bitcast.81, bf16[2048,4096]{1,0:T(8,128)(2,1)} %bitcast.76), custom_call_target="tpu_custom_call" | custom-call | flops 2147483648 | bytes 83886080 | tf_op jit(solution)/shard_map/relay_value_1/pallas_call | solution.py:211
  259.2 58.8 %relay_grad_0.1 = (bf16[256,4096]{1,0:T(8,128)(2,1)}, bf16[256,2048]{1,0:T(8,128)(2,1)}) custom-call(bf16[256,2048]{1,0:T(8,128)(2,1)} %all-gather.10.cloned.1.call-done.refs_0_, f32[256,2048]{1,0:T(8,128)} %get-tuple-element.26.refs_1_, f32[256,2048]{1,0:T(8,128)} %get-tuple-element.28.refs_2_, bf16[2048,4096]{1,0:T(8,128)(2,1)} %bitcast.77, ...), custom_call_target="tpu_custom_call" | custom-call | flops 8589934592 | bytes 167772160 | tf_op jit(solution)/shard_map/relay_grad_0/pallas_call | solution.py:211
  318.0 14.8 %fusion.1 = bf16[1,4096,2048]{2,1,0:T(8,128)(2,1)} fusion(bf16[256,2048]{1,0:T(8,128)(2,1)S(1)} %get-tuple-element.34, bf16[256,2048]{1,0:T(8,128)(2,1)S(1)} %get-tuple-element.33, bf16[256,4096]{1,0:T(8,128)(2,1)} %get-tuple-element.32, bf16[256,2048]{1,0:T(8,128)(2,1)} %all-gather.10.cloned.1.call-done.refs_0_, bf16[256,2048]{1,0:T(8,128)(2,1)} %bitcast.100), kind=kOutput, calls=%fused_computation.3 | convolution fusion | flops 8623489024 | bytes 23068672 | tf_op jit(solution)/shard_map/dot_general | solution.py:300
  332.9 14.2 %fusion = bf16[1,2048,4096]{2,1,0:T(8,128)(2,1)} fusion(bf16[256,4096]{1,0:T(8,128)(2,1)S(1)} %copy-done.5, bf16[256,4096]{1,0:T(8,128)(2,1)} %get-tuple-element.30, bf16[256,2048]{1,0:T(8,128)(2,1)S(1)} %bitcast.82, bf16[256,2048]{1,0:T(8,128)(2,1)} %bitcast.102), kind=kOutput, calls=%fused_computation.2 | convolution fusion | flops 8619294720 | bytes 23068672 | tf_op jit(solution)/shard_map/dot_general | solution.py:300
  347.1 1.2 fusion.37
  348.3 9.8 %all-reduce = (f32[64,1]{0,1:T(1,128)S(1)}, f32[64,1]{0,1:T(1,128)S(1)}) all-reduce(f32[64,1]{0,1:T(1,128)S(1)} %bitcast.97, f32[64,1]{0,1:T(1,128)S(1)} %bitcast.98), channel_id=1, replica_groups=mesh['section'=2,'dp'=4,'tensor'=4] {'dp'}, use_global_device_ids=true, to_apply=%region_13.14 | all-reduce | flops 128 | bytes 1024 | tf_op jit(solution)/shard_map/psum | solution.py:236
  358.2 5.2 %all-gather.4 = f32[4,2,2048]{2,1,0:T(2,128)S(1)} all-gather(f32[1,2,2048]{2,1,0:T(2,128)S(1)} %maximum_bitcast_fusion.1), channel_id=5, replica_groups=mesh['section'=2,'dp'=4,'tensor'=4] {'tensor'}, dimensions={0}, use_global_device_ids=true | all-gather | bytes 81920 | tf_op jit(solution)/shard_map/all_gather | solution.py:307
  364.1 1.1 fusion.38
  365.2 0.8 maximum_bitcast_fusion
  (38 shorter events, 2.5 us)
Async XLA Ops:
  7.2 21.8 %all-gather.16.cloned.1.call-start = ((), (), s32[]{:S(2)}) async-start(), calls=%async_computation.7 | async-start | bytes 1310720 | tf_op jit(solution)/shard_map/all_gather | solution.py:252
  7.9 40.0 %all-gather.14.cloned.1.call-start = ((), (), s32[]{:S(2)}) async-start(), calls=%async_computation.6 | async-start | bytes 1310720 | tf_op jit(solution)/shard_map/all_gather | solution.py:252
  26.1 139.9 %all-gather.12.cloned.1.call-start = ((), (), s32[]{:S(2)}) async-start(), calls=%async_computation.5 | async-start | bytes 1310720 | tf_op jit(solution)/shard_map/all_gather | solution.py:252
  26.9 177.7 %reduce-scatter.3.cloned.1.call-start = ((), (), s32[]{:S(2)}) async-start(), calls=%async_computation.2 | async-start | bytes 1310720 | tf_op jit(solution)/shard_map/reduce_scatter | solution.py:228
  166.1 93.1 %all-gather.10.cloned.1.call-start = ((), (), s32[]{:S(2)}) async-start(), calls=%async_computation.3 | async-start | bytes 1310720 | tf_op jit(solution)/shard_map/all_gather | solution.py:252
  166.2 38.5 %copy-start.4 = (f32[1,2048]{1,0:T(1,128)S(1)}, f32[1,2048]{1,0:T(1,128)}, u32[]{:S(2)}) copy-start(f32[1,2048]{1,0:T(1,128)} %param.10) | copy-start | bytes 24580
  166.2 49.3 %copy-start.2 = (bf16[1,64,2048]{2,1,0:T(8,128)(2,1)S(1)}, bf16[1,64,2048]{2,1,0:T(8,128)(2,1)}, u32[]{:S(2)}) copy-start(bf16[1,64,2048]{2,1,0:T(8,128)(2,1)} %param.8) | copy-start | bytes 786436
  166.2 58.7 %copy-start.3 = (bf16[64,2048]{1,0:T(8,128)(2,1)S(1)}, bf16[64,2048]{1,0:T(8,128)(2,1)}, u32[]{:S(2)}) copy-start(bf16[64,2048]{1,0:T(8,128)(2,1)} %param.9) | copy-start | bytes 786436
  216.7 8.3 %collective-permute-start = (bf16[64,2048]{1,0:T(8,128)(2,1)S(1)}, bf16[64,2048]{1,0:T(8,128)(2,1)S(1)}, u32[]{:S(2)}, u32[]{:S(2)}) collective-permute-start(bf16[64,2048]{1,0:T(8,128)(2,1)S(1)} %fusion.34), channel_id=1, source_target_pairs={{16,0},{17,1},{18,2},{19,3},{20,4},{21,5},{22,6},{23,7},{24,8},{25... | collective-permute-start | bytes 786440 | tf_op jit(solution)/shard_map/ppermute | solution.py:286
  225.7 121.4 %reduce-scatter.5.cloned.1.call-start = ((), (), s32[]{:S(2)}) async-start(), calls=%async_computation.4 | async-start | bytes 1310720 | tf_op jit(solution)/shard_map/reduce_scatter | solution.py:228
  318.0 14.9 %copy-start = (bf16[1,256,2048]{2,1,0:T(8,128)(2,1)S(1)}, bf16[1,256,2048]{2,1,0:T(8,128)(2,1)}, u32[]{:S(2)}) copy-start(bf16[1,256,2048]{2,1,0:T(8,128)(2,1)} %all-gather.12.cloned.1.call-done) | copy-start | bytes 3145732
  318.0 14.9 %copy-start.5 = (bf16[256,4096]{1,0:T(8,128)(2,1)S(1)}, bf16[256,4096]{1,0:T(8,128)(2,1)}, u32[]{:S(2)}) copy-start(bf16[256,4096]{1,0:T(8,128)(2,1)} %get-tuple-element.31) | copy-start | bytes 6291460
  332.8 31.2 %copy-start.1 = (bf16[64,2048]{1,0:T(8,128)(2,1)S(1)}, bf16[64,2048]{1,0:T(8,128)(2,1)}, u32[]{:S(2)}) copy-start(bf16[64,2048]{1,0:T(8,128)(2,1)} %broadcast_select_fusion) | copy-start | bytes 786436
Sparse Core Ops, SparseCore 0:
  9.6 19.4 all-gather.15
  31.1 16.7 all-gather.13
  50.0 16.7 all-gather.11
  166.2 24.7 reduce-scatter.2
  225.8 13.1 all-gather.9
  318.1 21.9 reduce-scatter.4
